TPU v7x, 256 devices: a whole 4x4x8 slice. The times are simulated.
256 devices in a mesh: row: 16 (over x, y), col: 16 (over z, core).
Axes of the slice: x: 4, y: 4, z: 8, core: 2. Of those that a mesh axis runs over, the one named last changes fastest.
Arguments:
- tiles: bfloat16 [64, 32, 128, 128], P('row', 'col'), may hold values from -6 to 6
- pattern: int32 [64, 32], P('row', 'col'), may hold values from -1 to 3, as said below
Outputs:
- sign_tiles: bfloat16 [64, 32, 128, 128], P('row', 'col')
- square_tiles: bfloat16 [64, 32, 128, 128], P('row', 'col')
Inputs may be any that keep to these rules, and one draw needn't show every extreme that they name: `pattern`: -1 marks an empty slot; the used block columns of one block row are distinct; the first slot of every panel is used, and every block row stores its diagonal block.
All inputs are finite; a program needn't handle non-finite values.
Results may differ from a plain program's by a relative error of at most 0.0058.
Values may be sent and summed in bfloat16 or wider, within the bound.
A program may use at most 64 MiB of HBM per device.

v0:
```python
import jax
import jax.numpy as jnp
from jax import lax
from jax.sharding import PartitionSpec as P

ITERS = 2


def pick_nonzero_blocks(kglob, piece_tiles, piece_layout, own_pat, start):
    count = piece_tiles.shape[0]
    group = jnp.arange(count, dtype=jnp.int32)
    row_hit = ((kglob - start)[:, :, None] == group[None, None, :]) & (kglob >= 0)[:, :, None]
    col_hit = (piece_layout[:, :, None, None] == own_pat[None, None, :, :]) & (piece_layout >= 0)[
        :, :, None, None
    ]
    col_hit = col_hit & (own_pat >= 0)[None, None, :, :]
    onehot = (
        row_hit[:, :, :, None, None] & jnp.transpose(col_hit, (2, 0, 1, 3))[:, None, :, :, :]
    ).astype(jnp.bfloat16)
    return jnp.einsum(
        "isgqt,gqbc->istbc", onehot, piece_tiles, preferred_element_type=jnp.float32
    ).astype(jnp.bfloat16)


def restricted(left_operand, kglob, right, pattern):
    panel_tiles, panel_layout = (
        lax.all_gather(right, "row", axis=0, tiled=True),
        lax.all_gather(pattern, "row", axis=0, tiled=True),
    )
    selected = pick_nonzero_blocks(kglob, panel_tiles, panel_layout, pattern, 0)
    return jnp.einsum(
        "isab,istbc->itac", left_operand, selected, preferred_element_type=jnp.float32
    )


def shards(tiles, pattern):
    rows_here, slots_here = pattern.shape
    n_row = lax.axis_size("row")
    n_col = lax.axis_size("col")
    panel_width = rows_here * n_row // n_col
    block = tiles.shape[-1]
    scale = 2.0 * slots_here * n_col * block
    valid = pattern >= 0
    keep = valid[:, :, None, None]
    sign = jnp.where(keep, tiles, jnp.zeros_like(tiles))
    square = sign
    for step in range(ITERS):
        left_operand, left_pat = (
            lax.all_gather(sign, "col", axis=1, tiled=True),
            lax.all_gather(pattern, "col", axis=1, tiled=True),
        )
        slot = jnp.arange(left_pat.shape[1], dtype=jnp.int32)
        kglob = jnp.where(left_pat >= 0, (slot // slots_here)[None, :] * panel_width + left_pat, -1)
        square = (restricted(left_operand, kglob, sign, pattern) / scale).astype(jnp.bfloat16)
        product = restricted(left_operand, kglob, square, pattern)
        sign = jnp.where(keep, 1.5 * sign.astype(jnp.float32) - 0.5 * product, 0.0).astype(
            jnp.bfloat16
        )
    return (sign, square)


def solution(mesh):
    return jax.shard_map(
        shards,
        mesh=mesh,
        in_specs=(P("row", "col", None, None), P("row", "col")),
        out_specs=(P("row", "col", None, None), P("row", "col", None, None)),
        check_vma=False,
    )
```

profile of v0, /device:TPU:2, one launch (start us, length us, event | category | flops | bytes accessed | tf_op | source)
XLA Modules:
  0.0 373.7 jit_solution(1548442793204792676)
XLA Ops:
  7.2 0.7 broadcast_compare_fusion.2
  8.0 1.1 copy.65
  9.2 0.9 copy.73
  10.2 0.9 copy.71
  11.1 0.8 copy.69
  11.8 23.3 %all-gather.1 = s32[16,4,2]{1,2,0:T(2,128)S(1)} all-gather(s32[1,4,2]{1,2,0:T(2,128)} %bitcast.164), channel_id=1, replica_groups=mesh['row'=16,'col'=16] {'row'}, dimensions={0}, use_global_device_ids=true | all-gather | bytes 544 | tf_op jit(solution)/shard_map/all_gather | solution.py:28
  35.2 20.2 %all-gather = s32[16,2,4]{2,1,0:T(2,128)S(1)} all-gather(s32[1,2,4]{2,1,0:T(2,128)} %bitcast.165), channel_id=1, replica_groups=mesh['row'=16,'col'=16] {'col'}, dimensions={0}, use_global_device_ids=true | all-gather | bytes 544 | tf_op jit(solution)/shard_map/all_gather | solution.py:50
  55.8 7.9 %copy.90 = bf16[4,32,128,128,1]{2,1,3,4,0:T(8,128)(2,1)} copy(bf16[4,32,128,128,1]{3,2,0,1,4:T(8,128)(2,1)} %bitcast.161) | data formatting | bytes 8388608 | tf_op jit(solution)/shard_map/all_gather | solution.py:49
  63.7 50.0 %all-gather.9.cloned.1.call-done = bf16[64,2,128,128]{3,2,1,0:T(8,128)(2,1)} async-done(((bf16[4,2,128,128]{3,2,1,0:T(8,128)(2,1)}), bf16[64,2,128,128]{3,2,1,0:T(8,128)(2,1)}) %all-gather.9.cloned.1.call-update) | async-done | bytes 4194320 | tf_op jit(solution)/shard_map/all_gather | solution.py:27
  113.7 9.2 %fusion.70 = bf16[4,2,128,128]{2,3,1,0:T(8,128)(2,1)S(1)} fusion(bf16[4,32,128,128,1]{2,1,3,4,0:T(8,128)(2,1)} %copy.90, bf16[64,2,128,128,1,1]{3,2,1,0,5,4:T(8,128)(2,1)} %bitcast.166, pred[4,64,2,2]{1,2,3,0:T(4,128)(4,1)S(1)} %and_and_fusion, pred[4,32,64]{2,1,0:T(8,128)(4,1)S(1)} %fusion.108), kind=kOutput, calls=%fused_computation.30 | convolution fusion | flops 2151972864 | bytes 8659968 | tf_op jit(solution)/shard_map/isab,istbc->itac/dot_general | solution.py:31
  122.9 0.9 copy.75
  124.0 56.2 %all-gather.13.cloned.1.call-done = bf16[64,2,128,128]{3,2,1,0:T(8,128)(2,1)} async-done(((bf16[4,2,128,128]{3,2,1,0:T(8,128)(2,1)}), bf16[64,2,128,128]{3,2,1,0:T(8,128)(2,1)}) %all-gather.13.cloned.1.call-update) | async-done | bytes 4194320 | tf_op jit(solution)/shard_map/all_gather | solution.py:27
  180.2 9.2 %fusion.67 = bf16[4,2,128,128]{2,3,1,0:T(8,128)(2,1)S(1)} fusion(bf16[4,32,128,128,1]{2,1,3,4,0:T(8,128)(2,1)} %copy.90, bf16[64,2,128,128,1,1]{3,2,1,0,5,4:T(8,128)(2,1)} %bitcast.168, pred[4,2]{1,0:T(4,128)(4,1)S(1)} %copy.64, pred[4,64,2,2]{1,2,3,0:T(4,128)(4,1)S(1)} %and_and_fusion, pred[4,32,64]{2,1,0:T(8,128)(4,1)S(1)} %fusion.108, ...), kind=kOutput, calls=%fused_computation.29 | convolution fusion | flops 2152628224 | bytes 8922120 | tf_op jit(solution)/shard_map/isab,istbc->itac/dot_general | solution.py:31
  189.4 0.9 copy.80
  190.3 0.9 copy.78
  191.2 0.3 all-gather.19.cloned.1.call-start
  191.5 40.8 %all-gather.17.cloned.1.call-done = bf16[4,32,128,128]{3,2,0,1:T(8,128)(2,1)} async-done(((bf16[4,2,128,128]{3,2,0,1:T(8,128)(2,1)}), bf16[4,32,128,128]{3,2,0,1:T(8,128)(2,1)}) %all-gather.17.cloned.1.call-update) | async-done | bytes 4194320 | tf_op jit(solution)/shard_map/all_gather | solution.py:49
  232.3 7.9 %copy.98 = bf16[4,32,128,128,1]{2,1,3,4,0:T(8,128)(2,1)} copy(bf16[4,32,128,128,1]{3,2,0,1,4:T(8,128)(2,1)} %bitcast.162) | data formatting | bytes 8388608 | tf_op jit(solution)/shard_map/all_gather | solution.py:49
  240.2 50.1 %all-gather.15.cloned.1.call-done = bf16[64,2,128,128]{3,2,1,0:T(8,128)(2,1)} async-done(((bf16[4,2,128,128]{3,2,1,0:T(8,128)(2,1)}), bf16[64,2,128,128]{3,2,1,0:T(8,128)(2,1)}) %all-gather.15.cloned.1.call-update) | async-done | bytes 4194320 | tf_op jit(solution)/shard_map/all_gather | solution.py:27
  290.3 9.2 %fusion.73 = bf16[4,2,128,128]{2,3,1,0:T(8,128)(2,1)S(1)} fusion(bf16[4,32,128,128,1]{2,1,3,4,0:T(8,128)(2,1)} %copy.98, bf16[64,2,128,128,1,1]{3,2,1,0,5,4:T(8,128)(2,1)} %bitcast.167, pred[4,64,2,2]{1,2,3,0:T(4,128)(4,1)S(1)} %and_and_fusion, pred[4,32,64]{2,1,0:T(8,128)(4,1)S(1)} %fusion.108), kind=kOutput, calls=%fused_computation.31 | convolution fusion | flops 2151972864 | bytes 8659968 | tf_op jit(solution)/shard_map/isab,istbc->itac/dot_general | solution.py:31
  299.5 0.9 copy.82
  300.3 56.4 %all-gather.19.cloned.1.call-done = bf16[64,2,128,128]{3,2,1,0:T(8,128)(2,1)} async-done(((bf16[4,2,128,128]{3,2,1,0:T(8,128)(2,1)}), bf16[64,2,128,128]{3,2,1,0:T(8,128)(2,1)}) %all-gather.19.cloned.1.call-update) | async-done | bytes 4194320 | tf_op jit(solution)/shard_map/all_gather | solution.py:27
  356.8 9.2 %fusion.64 = bf16[4,2,128,128]{2,3,1,0:T(8,128)(2,1)S(1)} fusion(bf16[4,32,128,128,1]{2,1,3,4,0:T(8,128)(2,1)} %copy.98, bf16[64,2,128,128,1,1]{3,2,1,0,5,4:T(8,128)(2,1)} %bitcast.169, bf16[4,2,128,128]{2,3,1,0:T(8,128)(2,1)S(1)} %fusion.67, pred[4,2]{1,0:T(4,128)(4,1)S(1)} %copy.64, pred[4,64,2,2]{1,2,3,0:T(4,128)(4,1)S(1)} %and_and_fusion, ...), kind=kOutput, calls=%fused_computation.28 | convolution fusion | flops 2152497152 | bytes 8922120 | tf_op jit(solution)/shard_map/isab,istbc->itac/dot_general | solution.py:31
  366.0 0.9 copy.85
  (22 shorter events, 1.1 us)
Async XLA Ops:
  7.2 48.6 %all-gather.11.cloned.1.call-start = ((), (), s32[]{:S(2)}) async-start(), calls=%async_computation.1 | async-start | bytes 4456448 | tf_op jit(solution)/shard_map/all_gather | solution.py:49
  10.1 103.6 %all-gather.9.cloned.1.call-start = ((), (), s32[]{:S(2)}) async-start(), calls=%async_computation | async-start | bytes 4456448 | tf_op jit(solution)/shard_map/all_gather | solution.py:27
  11.0 169.1 %all-gather.13.cloned.1.call-start = ((), (), s32[]{:S(2)}) async-start(), calls=%async_computation.2 | async-start | bytes 4456448 | tf_op jit(solution)/shard_map/all_gather | solution.py:27
  123.7 108.5 %all-gather.17.cloned.1.call-start = ((), (), s32[]{:S(2)}) async-start(), calls=%async_computation.4 | async-start | bytes 4456448 | tf_op jit(solution)/shard_map/all_gather | solution.py:49
  190.3 100.0 %all-gather.15.cloned.1.call-start = ((), (), s32[]{:S(2)}) async-start(), calls=%async_computation.3 | async-start | bytes 4456448 | tf_op jit(solution)/shard_map/all_gather | solution.py:27
  191.2 165.6 %all-gather.19.cloned.1.call-start = ((), (), s32[]{:S(2)}) async-start(), calls=%async_computation.5 | async-start | bytes 4456448 | tf_op jit(solution)/shard_map/all_gather | solution.py:27
Sparse Core Ops, SparseCore 0:
  10.4 44.8 all-gather.10
  58.3 55.3 all-gather.8
  123.9 56.2 all-gather.12
  190.4 41.8 all-gather.16
  235.1 55.1 all-gather.14
  300.5 56.2 all-gather.18
where the time goes:
time: 375 us; the launch traced here: 374 us
  waiting for transfers between devices  254 us (68%)
  blocking collectives  43.5 us (12%)
  matrix products  36.8 us (10%)
  local copies, waits for them, and re-layouts  23.9 us (6%)
  between operations  14.2 us (4%)
    all_gather x4, waiting for transfers between devices, restricted(): lax.all_gather(right, 'row', axis=0, tiled=True)  213 us
    all_gather x2, waiting for transfers between devices, shards(): lax.all_gather(sign, 'col', axis=1, tiled=True)  40.8 us
    dot_general x4, matrix products, restricted(): jnp.einsum('isab,istbc->itac', left_operand, selected, preferred_element_...  36.8 us
    all_gather x1, blocking collectives, restricted(): lax.all_gather(pattern, 'row', axis=0, tiled=True)  23.3 us
    all_gather x1, blocking collectives, shards(): lax.all_gather(pattern, 'col', axis=1, tiled=True)  20.2 us
    all_gather x2, local copies, waits for them, and re-layouts, shards(): lax.all_gather(sign, 'col', axis=1, tiled=True)  15.8 us
  transfers between devices with their start and end apart: 6, of which 5 were waited for; matrix products, arithmetic and copies ran while one was open for 5% of the time, Pallas kernels for 0%

commit v1 on v0

v1 whole, which is shorter than its diff:
```python
import functools

import jax
import jax.numpy as jnp
from jax import lax
from jax.experimental import pallas as pl
from jax.experimental.pallas import tpu as pltpu
from jax.sharding import PartitionSpec as P

ITERS = 2
SIDE = 4
RING = 8
LINES = 16
BLOCKS = 8
MESH = pl.DeviceIdType.MESH

PARTS = {"w": (0, 4), "a": (0, 2), "b": (2, 4)}
ROW_KEYS = []
for _h in (0, 1):
    ROW_KEYS += [(_h, -1, 0, "w"), (_h, 1, 0, "w"), (_h, 2, 0, "a"), (_h, 2, 0, "b")]
    for _f in (0, -1, 1, 2):
        ROW_KEYS += [(_h, _f, -1, "w"), (_h, _f, 1, "w"), (_h, _f, 2, "a"), (_h, _f, 2, "b")]
ROW_ID = {key: n for n, key in enumerate(ROW_KEYS)}

UP = [(1, 0, 1), (1, 1, 1), (1, 0, 2), (1, 1, 2), (1, 0, 3), (1, 1, 3), (1, 0, 4)]
DOWN = [(-1, 1, 1), (-1, 0, 1), (-1, 1, 2), (-1, 0, 2), (-1, 1, 3), (-1, 0, 3), (-1, 1, 4)]
COL_KEYS = UP + DOWN + [("c", 0, 0, 0)] + [("c",) + key for key in UP + DOWN]
COL_ID = {key: n for n, key in enumerate(COL_KEYS)}


def kernel(
    tiles, pattern, sign_out, square_out,
    left, right, loc, acc, prow, pcol, srow, scol, table,
    psend, precv, plocal, rsend, rrecv, csend, crecv,
):
    row, col = lax.axis_index("row"), lax.axis_index("col")
    x, y = lax.div(row, SIDE), lax.rem(row, SIDE)
    z, core = lax.div(col, 2), lax.rem(col, 2)

    def row_at(dx, dy):
        return lax.rem(x + dx + SIDE, SIDE) * SIDE + lax.rem(y + dy + SIDE, SIDE)

    def col_at(dz, own_core=True):
        return lax.rem(z + dz + RING, RING) * 2 + (core if own_core else 1 - core)

    def row_copy(half, key, sending):
        h, f, s, part = key
        second = s != 0
        step = {-1: 1, 1: -1}.get(s if second else f) or (1 if part == "a" else -1)
        if sending:
            if second:
                s = s + step if s != 2 else -step
            else:
                f = f + step if f != 2 else -step
        lo, hi = PARTS[part]
        off = (f, s) if h == 0 else (s, f)
        ref = right.at[half, row_at(*off), pl.ds(h * 4 + lo, hi - lo)]
        to_x = (h == 0) != second
        target = row_at(step, 0) if to_x else row_at(0, step)
        n = ROW_ID[key]
        return pltpu.make_async_remote_copy(
            src_ref=ref, dst_ref=ref, send_sem=rsend.at[half, n], recv_sem=rrecv.at[half, n],
            device_id=(target, col), device_id_type=MESH,
        )

    def row_send(half, *keys):
        for key in keys:
            row_copy(half, key, True).start()

    def row_wait(half, *keys):
        for key in keys:
            row_copy(half, key, False).wait_recv()

    def col_copy(it, key, sending):
        if key[0] == "c":
            _, sign, h, d = key
            ref_col = col_at(-sign * d, sending)
            target = col_at(0, False)
            lo, n = (0, 8) if d == 0 else (h * 4, 4)
        else:
            sign, h, d = key
            ref_col = col_at(-sign * (d - 1 if sending else d))
            target = col_at(sign)
            lo, n = h * 4, 4
        ref = left.at[it, ref_col, pl.ds(lo, n)]
        k = COL_ID[key]
        return pltpu.make_async_remote_copy(
            src_ref=ref, dst_ref=ref, send_sem=csend.at[it, k], recv_sem=crecv.at[it, k],
            device_id=(row, target), device_id_type=MESH,
        )

    def col_send(it, *keys):
        for key in keys:
            col_copy(it, key, True).start()

    def col_event(it, n):
        for key in (UP[n], DOWN[n]):
            col_copy(it, key, False).wait_recv()
            sign, h, d = key
            if (sign, h, d + 1) in COL_ID:
                col_send(it, (sign, h, d + 1))
            col_send(it, ("c",) + key)

    def cross_wait(it, least, most):
        for key in COL_KEYS:
            if key[0] == "c" and least <= key[3] <= most:
                col_copy(it, key, False).wait_recv()

    def row_start(half):
        for h in (0, 1):
            row_send(half, (h, -1, 0, "w"), (h, 1, 0, "w"))
        for h in (1, 0):
            row_send(half, (h, 0, -1, "w"), (h, 0, 1, "w"))

    def row_e1(half):
        for h in (0, 1):
            for f, part in ((-1, "a"), (1, "b")):
                row_wait(half, (h, f, 0, "w"))
                row_send(half, (h, 2, 0, part), (h, f, -1, "w"), (h, f, 1, "w"))

    def row_fan(half, f):
        for h in (0, 1):
            for s, part in ((-1, "a"), (1, "b")):
                row_wait(half, (h, f, s, "w"))
                row_send(half, (h, f, 2, part))

    def row_e3(half):
        for h in (0, 1):
            row_wait(half, (h, 2, 0, "a"), (h, 2, 0, "b"))
            row_send(half, (h, 2, -1, "w"), (h, 2, 1, "w"))

    def row_last(half, *fs):
        for f in fs:
            for h in (0, 1):
                row_wait(half, (h, f, 2, "a"), (h, f, 2, "b"))

    def piece(it, half, r):
        loc[0:BLOCKS] = right[half, r]
        for i in range(4):
            at = r * 16 + i * 4
            a = jnp.concatenate([left[it, r, 2 * i], left[it, r, 2 * i + 1]], axis=1)
            b = jnp.concatenate(
                [
                    jnp.concatenate([loc[table[at + 2 * s]], loc[table[at + 2 * s + 1]]], axis=1)
                    for s in (0, 1)
                ],
                axis=0,
            )
            acc[i] += jnp.dot(a, b, preferred_element_type=jnp.float32)

    def make_table(first, count):
        @pl.loop(first, first + count)
        def _(r):
            for i in range(4):
                for s in range(2):
                    k = scol[r, i, s]
                    at_k = jnp.maximum(k, 0)
                    j0, j1 = srow[r, at_k, 0], srow[r, at_k, 1]
                    for t in range(2):
                        j = srow[row, i, t]
                        ok = (k >= 0) & (j >= 0)
                        found = jnp.where(j0 == j, 2 * at_k, jnp.where(j1 == j, 2 * at_k + 1, BLOCKS))
                        table[r * 16 + i * 4 + s * 2 + t] = jnp.where(ok, found, BLOCKS)

    def patterns():
        for land, smem, n in ((prow, srow, 0), (pcol, scol, 1)):
            some = land.at[pl.ds(0, LINES - 1)]
            pltpu.make_async_copy(some, some, precv.at[n]).wait()
            pltpu.make_async_copy(land, smem, plocal.at[n]).start()
        for land, smem, n in ((prow, srow, 0), (pcol, scol, 1)):
            pltpu.make_async_copy(land, smem, plocal.at[n]).wait()

    padded = jnp.full((8, 128), -1, jnp.int32)
    prow[row] = padded
    pcol[col] = padded
    prow[row, 0:4, 0:2] = pattern[...]
    pcol[col, 0:4, 0:2] = pattern[...]
    own = tiles[...].reshape(BLOCKS, 128, 128)
    left[0, col] = own
    right[0, row] = own
    loc[BLOCKS] = jnp.zeros((128, 128), jnp.bfloat16)

    barrier = pltpu.get_barrier_semaphore()

    @pl.loop(1, LINES)
    def _(d):
        pl.semaphore_signal(barrier, inc=1, device_id=(lax.rem(row + d, LINES), col), device_id_type=MESH)
        pl.semaphore_signal(barrier, inc=1, device_id=(row, lax.rem(col + d, LINES)), device_id_type=MESH)

    pl.semaphore_wait(barrier, 2 * (LINES - 1))

    def pattern_copy(d, n):
        land = (prow.at[row], pcol.at[col])[n]
        to = ((lax.rem(row + d, LINES), col), (row, lax.rem(col + d, LINES)))[n]
        return pltpu.make_async_remote_copy(
            src_ref=land, dst_ref=land, send_sem=psend.at[n], recv_sem=precv.at[n],
            device_id=to, device_id_type=MESH,
        )

    @pl.loop(0, ITERS)
    def _(it):
        first, second = 2 * it, 2 * it + 1

        row_start(first)
        col_send(it, UP[0], DOWN[0], UP[1], DOWN[1], ("c", 0, 0, 0))

        @pl.when(it == 0)
        def _():
            @pl.loop(1, LINES)
            def _(d):
                pattern_copy(d, 0).start()
                pattern_copy(d, 1).start()

        acc[...] = jnp.zeros_like(acc)
        row_e1(first)
        col_event(it, 0)
        row_fan(first, 0)
        col_event(it, 1)

        @pl.when(it == 0)
        def _():
            patterns()
            make_table(0, 8)

        row_e3(first)
        col_event(it, 2)

        @pl.when(it == 0)
        def _():
            make_table(8, 8)

        row_fan(first, -1)
        col_event(it, 3)
        row_fan(first, 1)
        col_event(it, 4)
        row_last(first, 0)
        col_event(it, 5)
        row_fan(first, 2)
        col_event(it, 6)
        row_last(first, -1, 1, 2)
        cross_wait(it, 0, 4)

        @pl.loop(0, LINES)
        def _(r):
            piece(it, first, r)

        scale = 1.0 / (2.0 * 2 * LINES * 128)
        for i in range(4):
            for t in range(2):
                block = acc[i, :, t * 128 : (t + 1) * 128]
                right[second, row, 2 * i + t] = (block * scale).astype(jnp.bfloat16)

        row_start(second)
        acc[...] = jnp.zeros_like(acc)
        row_e1(second)
        row_fan(second, 0)

        @pl.loop(0, 3)
        def _(n):
            piece(it, second, row_at(n - 1, 0))

        row_e3(second)

        @pl.loop(0, 2)
        def _(n):
            piece(it, second, row_at(0, 2 * n - 1))

        row_fan(second, -1)
        row_fan(second, 1)

        @pl.loop(0, 4)
        def _(n):
            piece(it, second, row_at(lax.div(n, 2) * 2 - 1, lax.rem(n, 2) * 2 - 1))

        row_last(second, 0)
        row_fan(second, 2)

        @pl.loop(0, 2)
        def _(n):
            piece(it, second, row_at(2 * n, 2 - 2 * n))

        row_last(second, -1, 1)

        @pl.loop(0, 2)
        def _(n):
            piece(it, second, row_at(2, 2 * n - 1))

        @pl.loop(0, 2)
        def _(n):
            piece(it, second, row_at(2 * n - 1, 2))

        row_last(second, 2)
        piece(it, second, row_at(2, 2))

        for i in range(4):
            for t in range(2):
                s = left[it, col, 2 * i + t].astype(jnp.float32)
                new = 1.5 * s - 0.5 * acc[i, :, t * 128 : (t + 1) * 128]
                keep = srow[row, i, t] >= 0
                new = jnp.where(keep, new, 0.0).astype(jnp.bfloat16)
                sign_out[i, t] = new

        @pl.when(it < ITERS - 1)
        def _():
            now = sign_out[...].reshape(BLOCKS, 128, 128)
            left[it + 1, col] = now
            right[2 * it + 2, row] = now

        for key in ROW_KEYS:
            row_copy(first, key, True).wait_send()
            row_copy(second, key, True).wait_send()
        for key in COL_KEYS:
            col_copy(it, key, True).wait_send()

    square_out[...] = right[2 * ITERS - 1, row].reshape(4, 2, 128, 128)
    for land, n in ((prow, 0), (pcol, 1)):
        some = land.at[pl.ds(0, LINES - 1)]
        pltpu.make_async_copy(some, some, psend.at[n]).wait()


def shards(tiles, pattern):
    shape = jax.ShapeDtypeStruct(tiles.shape, tiles.dtype)
    vmem = pl.BlockSpec(memory_space=pltpu.VMEM)
    dma = pltpu.SemaphoreType.DMA
    return pl.pallas_call(
        kernel,
        out_shape=(shape, shape),
        in_specs=[vmem, vmem],
        out_specs=(vmem, vmem),
        scratch_shapes=[
            pltpu.VMEM((ITERS, LINES, BLOCKS, 128, 128), jnp.bfloat16),
            pltpu.VMEM((2 * ITERS, LINES, BLOCKS, 128, 128), jnp.bfloat16),
            pltpu.VMEM((BLOCKS + 1, 128, 128), jnp.bfloat16),
            pltpu.VMEM((4, 128, 256), jnp.float32),
            pltpu.VMEM((LINES, 8, 128), jnp.int32),
            pltpu.VMEM((LINES, 8, 128), jnp.int32),
            pltpu.SMEM((LINES, 8, 128), jnp.int32),
            pltpu.SMEM((LINES, 8, 128), jnp.int32),
            pltpu.SMEM((LINES * 16,), jnp.int32),
            dma((2,)),
            dma((2,)),
            dma((2,)),
            dma((2 * ITERS, len(ROW_KEYS))),
            dma((2 * ITERS, len(ROW_KEYS))),
            dma((ITERS, len(COL_KEYS))),
            dma((ITERS, len(COL_KEYS))),
        ],
        compiler_params=pltpu.CompilerParams(
            collective_id=0, has_side_effects=True, vmem_limit_bytes=48 * 1024 * 1024
        ),
    )(tiles, pattern)


def solution(mesh):
    return jax.shard_map(
        shards,
        mesh=mesh,
        in_specs=(P("row", "col", None, None), P("row", "col")),
        out_specs=(P("row", "col", None, None), P("row", "col", None, None)),
        check_vma=False,
    )
```

time: 375 us -> 131 us (0.35)
  waiting for transfers between devices: 254 us -> 0 us
  Pallas kernels: 0 us -> 126 us
  blocking collectives: 43.5 us -> 0 us
  matrix products: 36.8 us -> 0 us
  local copies, waits for them, and re-layouts: 23.9 us -> 3.12 us
  between operations: 14.2 us -> 0.64 us
    all_gather x6 -> x0, waiting for transfers between devices: 254 us -> none  [the longest x4 213 us: restricted(): lax.all_gather(right, 'row', axis=0, tiled=True)]
    pallas_call x0 -> x1, Pallas kernels: none -> 126 us  [shards(): pl.pallas_call(kernel, out_shape=(shape, shape), in_specs=[vmem, vmem], o...]
    all_gather x2 -> x0, blocking collectives: 43.5 us -> none  [the longest x1 23.3 us: restricted(): lax.all_gather(pattern, 'row', axis=0, tiled=True)]
    dot_general x4 -> x0, matrix products: 36.8 us -> none  [restricted(): jnp.einsum('isab,istbc->itac', left_operand, selected, preferred_element_...]
    all_gather x3 -> x0, local copies, waits for them, and re-layouts: 15.8 us -> none  [the longest x2 15.8 us: shards(): lax.all_gather(sign, 'col', axis=1, tiled=True)]
  transfers between devices with their start and end apart: 6 -> 0, of which waited for: 5 -> 0; matrix products, arithmetic and copies ran while one was open for 5% -> 0% of each run, Pallas kernels for 0% -> 0%
where the time goes in v1:
time: 131 us; the launch traced here: 130 us
  Pallas kernels  126 us (96%)
  local copies, waits for them, and re-layouts  3.12 us (2%)
    pallas_call x1, Pallas kernels, shards(): pl.pallas_call(kernel, out_shape=(shape, shape), in_specs=[vmem, vmem], o...  126 us
    unnamed x5, local copies, waits for them, and re-layouts  3.12 us

profile of v1, /device:TPU:2, one launch (start us, length us, event | category | flops | bytes accessed | tf_op | source)
XLA Modules:
  0.0 130.2 jit_solution(10603286739429888816)
XLA Ops:
  0.6 0.8 copy.4.pattern
  1.4 0.0 copy-start
  1.4 0.9 copy-done
  2.3 126.5 %shard_map.41 = (bf16[4,2,128,128]{3,2,1,0:T(8,128)(2,1)S(1)}, bf16[4,2,128,128]{3,2,1,0:T(8,128)(2,1)S(1)}) custom-call(bf16[4,2,128,128]{3,2,1,0:T(8,128)(2,1)S(1)} %copy-done, s32[4,2]{1,0:T(4,128)S(1)} %copy.4.pattern), custom_call_target="tpu_custom_call" | custom-call | tf_op jit(solution)/shard_map/pallas_call | solution.py:325
  128.8 0.7 copy.7
  129.5 0.7 copy.8
Async XLA Ops:
  1.4 0.9 copy-start

commit v2 on v0

v2 whole, which is shorter than its diff:
```python
import jax
import jax.numpy as jnp
from jax import lax
from jax.experimental import pallas as pl
from jax.experimental.pallas import tpu as pltpu
from jax.sharding import PartitionSpec as P

ITERS = 2
SIDE = 4
RING = 8
LINES = 16
BLOCKS = 8
BS = 128
GROUP = 4
HEAD = 16
ROWS = BLOCKS * BS
MESH = pl.DeviceIdType.MESH

PARTS = {"w": (0, 4), "a": (0, 2), "b": (2, 4)}
ROW_KEYS = []
for _h in (0, 1):
    ROW_KEYS += [(_h, -1, 0, "w"), (_h, 1, 0, "w"), (_h, 2, 0, "a"), (_h, 2, 0, "b")]
    for _f in (0, -1, 1, 2):
        ROW_KEYS += [(_h, _f, -1, "w"), (_h, _f, 1, "w"), (_h, _f, 2, "a"), (_h, _f, 2, "b")]
ROW_ID = {key: n for n, key in enumerate(ROW_KEYS)}

UP = [(1, q, d) for d in (1, 2, 3) for q in (0, 1, 2, 3)] + [(1, q, 4) for q in (0, 1)]
DOWN = [(-1, q, d) for d in (1, 2, 3) for q in (2, 3, 0, 1)] + [(-1, q, 4) for q in (2, 3)]
CROSS = [("c", 1, 0)] + [("c", s, d) for d in (1, 2, 3, 4) for s in (1, -1)]
COL_ID = {key: n for n, key in enumerate(UP + DOWN + CROSS)}


def kernel(
    tiles, pattern, sign_out, square_out,
    left, right, mid, loc, acc, pv, table, used,
    tsem, psem, rsend, rrecv, csend, crecv,
):
    row, col = lax.axis_index("row"), lax.axis_index("col")
    x, y = lax.div(row, SIDE), lax.rem(row, SIDE)
    z, core = lax.div(col, 2), lax.rem(col, 2)

    def row_at(dx, dy):
        return lax.rem(x + dx + SIDE, SIDE) * SIDE + lax.rem(y + dy + SIDE, SIDE)

    def col_at(dz, own_core=True):
        return lax.rem(z + dz + RING, RING) * 2 + (core if own_core else 1 - core)

    def block(n):
        return pl.ds(HEAD + n * BS, BS)

    def row_copy(it, which, key, sending):
        h, f, s, part = key
        second = s != 0
        step = {-1: 1, 1: -1}.get(s if second else f) or (1 if part == "a" else -1)
        if sending:
            if second:
                s = s + step if s != 2 else -step
            else:
                f = f + step if f != 2 else -step
        lo, hi = ((h * 4 + p) * BS for p in PARTS[part])
        off = (f, s) if h == 0 else (s, f)
        if which == 0:
            lo, hi = lo + HEAD if lo else 0, hi + HEAD
        ref = (right, mid)[which].at[it, row_at(*off), pl.ds(lo, hi - lo)]
        target = row_at(step, 0) if (h == 0) != second else row_at(0, step)
        return pltpu.make_async_remote_copy(
            src_ref=ref, dst_ref=ref, send_sem=rsend.at[it, which], recv_sem=rrecv.at[it, which, ROW_ID[key]],
            device_id=(target, col), device_id_type=MESH,
        )

    def row_send(g, *keys):
        for key in keys:
            row_copy(*g, key, True).start()

    def row_wait(g, *keys):
        for key in keys:
            row_copy(*g, key, False).wait_recv()

    def col_copy(it, key, sending):
        sign, d = key[-3] if key[0] != "c" else key[1], key[-1]
        if key[0] == "c":
            ref_col = col_at(-sign * d, sending)
            target = col_at(0, False)
            lo, hi = (0, 4) if d < 4 else ((0, 2) if sign == 1 else (2, 4))
        else:
            ref_col = col_at(-sign * (d - 1 if sending else d))
            target = col_at(sign)
            lo, hi = key[1], key[1] + 1
        lo, hi = lo * 2 * BS + HEAD if lo else 0, hi * 2 * BS + HEAD
        ref = left.at[it, ref_col, pl.ds(lo, hi - lo)]
        return pltpu.make_async_remote_copy(
            src_ref=ref, dst_ref=ref, send_sem=csend.at[it], recv_sem=crecv.at[it, COL_ID[key]],
            device_id=(row, target), device_id_type=MESH,
        )

    def col_start(it):
        for up, down in zip(UP[:4], DOWN[:4]):
            col_copy(it, up, True).start()
            col_copy(it, down, True).start()
        col_copy(it, CROSS[0], True).start()

    def col_event(it, *ns):
        for n in ns:
            for key in (UP[n], DOWN[n]):
                col_copy(it, key, False).wait_recv()
                sign, q, d = key
                if (sign, q, d + 1) in COL_ID:
                    col_copy(it, (sign, q, d + 1), True).start()
                if n % 4 == 3 or n == 13:
                    col_copy(it, ("c", sign, d), True).start()

    def cross_wait(it, *ds):
        for key in CROSS:
            if key[2] in ds:
                col_copy(it, key, False).wait_recv()

    def row_start(g):
        for h in (0, 1):
            row_send(g, (h, -1, 0, "w"), (h, 1, 0, "w"))
        for h in (1, 0):
            row_send(g, (h, 0, -1, "w"), (h, 0, 1, "w"))

    def row_e1(g):
        for h in (0, 1):
            for f, part in ((-1, "a"), (1, "b")):
                row_wait(g, (h, f, 0, "w"))
                row_send(g, (h, 2, 0, part))
        for f in (-1, 1):
            for h in (0, 1):
                row_send(g, (h, f, -1, "w"), (h, f, 1, "w"))

    def row_e3(g):
        for h in (0, 1):
            row_wait(g, (h, 2, 0, "a"), (h, 2, 0, "b"))
            row_send(g, (h, 2, -1, "w"), (h, 2, 1, "w"))

    def row_fan(g, f):
        for h in (1, 0):
            for s, part in ((-1, "a"), (1, "b")):
                row_wait(g, (h, f, s, "w"))
                row_send(g, (h, f, 2, part))

    def row_last(g, *fs):
        for f in fs:
            for h in (0, 1):
                row_wait(g, (h, f, 2, "a"), (h, f, 2, "b"))

    def sent(ref, sem):
        some = ref.at[0, pl.ds(0, LINES - 1)]
        pltpu.make_async_copy(some, some, sem).wait()

    def pieces(it, which, rs):
        head = HEAD if which == 0 else 0
        for g, r in enumerate(rs):
            for n in range(BLOCKS):
                loc[g, n] = (right, mid)[which][it, r, pl.ds(head + n * BS, BS)]
            for i in range(4):
                a = jnp.concatenate([left[it, r, block(2 * i)], left[it, r, block(2 * i + 1)]], axis=1)
                b = [[loc[g, table[r, 4 * i + 2 * s + t]] for t in (0, 1)] for s in (0, 1)]
                b = jnp.concatenate([jnp.concatenate(pair, axis=1) for pair in b], axis=0)
                acc[i] += jnp.dot(a, b, preferred_element_type=jnp.float32)

    def apart(a, b, n):
        d = lax.rem(a - b + n, n)
        return jnp.minimum(d, n - d)

    def decode(tile):
        at = lax.broadcasted_iota(jnp.int32, (HEAD, BS), 0)
        entry = tile.astype(jnp.float32).astype(jnp.int32) + 1
        code = jnp.where(at < BLOCKS, entry << (3 * jnp.minimum(at, BLOCKS - 1)), 0)
        return jnp.sum(code, axis=0, keepdims=True)

    def make_table():
        for r in range(LINES):
            pv[0, r : r + 1] = decode(right[0, r, 0:HEAD])
            pv[1, r : r + 1] = decode(left[0, r, 0:HEAD])
        theirs, mine = pv[0], pv[1]
        own = jnp.broadcast_to(decode(left[0, col, 0:HEAD]), (LINES, BS))
        lane = lax.broadcasted_iota(jnp.int32, (LINES, BS), 1) & 15
        i, s, t = lane >> 2, (lane >> 1) & 1, lane & 1
        k = ((mine >> (6 * i + 3 * s)) & 7) - 1
        at_k = jnp.clip(k, 0, SIDE - 1)
        pair = theirs >> (6 * at_k)
        j = (own >> (6 * i + 3 * t)) & 7
        found = jnp.where((pair & 7) == j, 2 * at_k, jnp.where(((pair >> 3) & 7) == j, 2 * at_k + 1, BLOCKS))
        pv[2] = jnp.where((k >= 0) & (j > 0), found, BLOCKS)
        pv[3] = j
        copies = [pltpu.make_async_copy(pv.at[2 + n], (table, used)[n], psem.at[n]) for n in (0, 1)]
        for copy in copies:
            copy.start()
        for copy in copies:
            copy.wait()

    barrier = pltpu.get_barrier_semaphore()
    for peer in (
        (row_at(1, 0), col), (row_at(-1, 0), col), (row_at(0, 1), col), (row_at(0, -1), col),
        (row, col_at(1)), (row, col_at(-1)), (row, col_at(0, False)),
    ):
        pl.semaphore_signal(barrier, inc=1, device_id=peer, device_id_type=MESH)

    body = pl.ds(HEAD, ROWS)
    fetch = [
        pltpu.make_async_copy(tiles, right.at[0, row, body], tsem.at[0]),
        pltpu.make_async_copy(tiles, left.at[0, col, body], tsem.at[1]),
    ]
    for copy in fetch:
        copy.start()
    n_row = lax.broadcasted_iota(jnp.int32, (HEAD, BS), 0)
    head = jnp.zeros((HEAD, BS), jnp.float32)
    for n in range(BLOCKS):
        entry = jnp.broadcast_to(pattern[n % 2 : n % 2 + 1, n // 2 : n // 2 + 1], (HEAD, BS)).astype(jnp.float32)
        head = jnp.where(n_row == n, entry, head)
    for it in range(ITERS):
        right[it, row, 0:HEAD] = head.astype(jnp.bfloat16)
        left[it, col, 0:HEAD] = head.astype(jnp.bfloat16)
    for k in range(GROUP):
        loc[k, BLOCKS] = jnp.zeros((BS, BS), jnp.bfloat16)

    early, order = jnp.int32(0), [jnp.int32(0)] * (LINES // GROUP)
    for r in range(LINES):
        dx, dy, dz = apart(r // SIDE, x, SIDE), apart(r % SIDE, y, SIDE), apart(r // 2, z, RING)
        soon = jnp.where((dx + dy <= 2) & (dz <= 3), 1, 0)
        at = jnp.where(soon == 1, early, LINES - 1 - r + early)
        early = early + soon
        for k in range(LINES // GROUP):
            for j in range(GROUP):
                order[k] = order[k] + jnp.where(at == k * GROUP + j, r * 16**j, 0)

    def group(k):
        word = order[0]
        for n in range(1, LINES // GROUP):
            word = jnp.where(k == n, order[n], word)
        return [lax.rem(lax.div(word, 16**j), 16) for j in range(GROUP)]

    for copy in fetch:
        copy.wait()
    pl.semaphore_wait(barrier, 7)

    @pl.loop(0, ITERS)
    def _(it):
        g, m = (it, 0), (it, 1)

        row_start(g)
        col_start(it)
        acc[...] = jnp.zeros_like(acc)
        col_event(it, 0, 1)
        row_e1(g)
        col_event(it, 2, 3)
        row_e3(g)
        col_event(it, 4, 5, 6)
        row_fan(g, -1)
        col_event(it, 7, 8)
        row_fan(g, 1)
        col_event(it, 9, 10, 11)
        row_fan(g, 0)
        row_fan(g, 2)
        col_event(it, 12, 13)
        row_last(g, 0)
        cross_wait(it, 0, 1, 2, 3)

        @pl.when(it > 0)
        def _():
            @pl.loop(0, 2)
            def _(k):
                pieces(it, 0, group(k))

        row_last(g, -1, 1, 2)
        cross_wait(it, 4)

        @pl.when(it == 0)
        def _():
            make_table()

        @pl.loop(jnp.where(it == 0, 0, 2), 4)
        def _(k):
            pieces(it, 0, group(k))

        scale = 1.0 / (2.0 * 2 * LINES * BS)
        for i in range(4):
            for t in range(2):
                new = acc[i, :, t * BS : (t + 1) * BS] * scale
                mid[it, row, pl.ds((2 * i + t) * BS, BS)] = new.astype(jnp.bfloat16)

        row_start(m)
        acc[...] = jnp.zeros_like(acc)
        row_e1(m)
        row_e3(m)
        row_fan(m, 0)
        row_fan(m, -1)
        pieces(it, 1, [row_at(0, 0), row_at(-1, 0), row_at(1, 0)])
        row_fan(m, 1)
        pieces(it, 1, [row_at(0, -1), row_at(0, 1)])
        row_fan(m, 2)
        pieces(it, 1, [row_at(-1, -1), row_at(-1, 1), row_at(1, -1), row_at(1, 1)])
        row_last(m, 0)
        pieces(it, 1, [row_at(2, 0), row_at(0, 2)])
        for f in (-1, 1):
            row_last(m, f)
            pieces(it, 1, [row_at(2, f), row_at(f, 2)])
        row_last(m, 2)
        pieces(it, 1, [row_at(2, 2)])

        for i in range(4):
            for t in range(2):
                s = left[it, col, block(2 * i + t)].astype(jnp.float32)
                new = 1.5 * s - 0.5 * acc[i, :, t * BS : (t + 1) * BS]
                keep = used[0, 4 * i + t] > 0
                sign_out[i, t] = jnp.where(keep, new, 0.0).astype(jnp.bfloat16)

        @pl.when(it < ITERS - 1)
        def _():
            for n in range(BLOCKS):
                now = sign_out[n // 2, n % 2]
                left[it + 1, col, block(n)] = now
                right[it + 1, row, block(n)] = now

    for n in range(BLOCKS):
        square_out[n // 2, n % 2] = mid[ITERS - 1, row, pl.ds(n * BS, BS)]
    for it in range(ITERS):
        sent(right, rsend.at[it, 0])
        sent(mid, rsend.at[it, 1])
        sent(left, csend.at[it])


def shards(tiles, pattern):
    shape = jax.ShapeDtypeStruct(tiles.shape, tiles.dtype)
    vmem = pl.BlockSpec(memory_space=pltpu.VMEM)
    dma = pltpu.SemaphoreType.DMA
    return pl.pallas_call(
        kernel,
        out_shape=(shape, shape),
        in_specs=[pl.BlockSpec(memory_space=pltpu.HBM), vmem],
        out_specs=(vmem, vmem),
        scratch_shapes=[
            pltpu.VMEM((ITERS, LINES, HEAD + ROWS, BS), jnp.bfloat16),
            pltpu.VMEM((ITERS, LINES, HEAD + ROWS, BS), jnp.bfloat16),
            pltpu.VMEM((ITERS, LINES, ROWS, BS), jnp.bfloat16),
            pltpu.VMEM((GROUP, BLOCKS + 1, BS, BS), jnp.bfloat16),
            pltpu.VMEM((4, BS, 2 * BS), jnp.float32),
            pltpu.VMEM((4, LINES, BS), jnp.int32),
            pltpu.SMEM((LINES, BS), jnp.int32),
            pltpu.SMEM((LINES, BS), jnp.int32),
            dma((2,)),
            dma((2,)),
            dma((ITERS, 2)),
            dma((ITERS, 2, len(ROW_KEYS))),
            dma((ITERS,)),
            dma((ITERS, len(COL_ID))),
        ],
        compiler_params=pltpu.CompilerParams(
            collective_id=0, has_side_effects=True, vmem_limit_bytes=48 * 1024 * 1024
        ),
    )(tiles.reshape(ROWS, BS), pattern.T)


def solution(mesh):
    return jax.shard_map(
        shards,
        mesh=mesh,
        in_specs=(P("row", "col", None, None), P("row", "col")),
        out_specs=(P("row", "col", None, None), P("row", "col", None, None)),
        check_vma=False,
    )
```

time: 375 us -> 112 us (0.30)
  waiting for transfers between devices: 254 us -> 0 us
  Pallas kernels: 0 us -> 108 us
  blocking collectives: 43.5 us -> 0 us
  matrix products: 36.8 us -> 0 us
  local copies, waits for them, and re-layouts: 23.9 us -> 3.03 us
  between operations: 14.2 us -> 0.65 us
    all_gather x6 -> x0, waiting for transfers between devices: 254 us -> none  [the longest x4 213 us: restricted(): lax.all_gather(right, 'row', axis=0, tiled=True)]
    pallas_call x0 -> x1, Pallas kernels: none -> 108 us  [shards(): pl.pallas_call(kernel, out_shape=(shape, shape), in_specs=[pl.BlockSpec(m...]
    all_gather x2 -> x0, blocking collectives: 43.5 us -> none  [the longest x1 23.3 us: restricted(): lax.all_gather(pattern, 'row', axis=0, tiled=True)]
    dot_general x4 -> x0, matrix products: 36.8 us -> none  [restricted(): jnp.einsum('isab,istbc->itac', left_operand, selected, preferred_element_...]
    all_gather x3 -> x0, local copies, waits for them, and re-layouts: 15.8 us -> none  [the longest x2 15.8 us: shards(): lax.all_gather(sign, 'col', axis=1, tiled=True)]
  transfers between devices with their start and end apart: 6 -> 0, of which waited for: 5 -> 0; matrix products, arithmetic and copies ran while one was open for 5% -> 0% of each run, Pallas kernels for 0% -> 0%
where the time goes in v2:
time: 112 us
  Pallas kernels  108 us (96%)
  local copies, waits for them, and re-layouts  3.03 us (3%)
    pallas_call x1, Pallas kernels, shards(): pl.pallas_call(kernel, out_shape=(shape, shape), in_specs=[pl.BlockSpec(m...  108 us
    unnamed x6, local copies, waits for them, and re-layouts  3.03 us

profile of v2, /device:TPU:2, one launch (start us, length us, event | category | flops | bytes accessed | tf_op | source)
XLA Modules:
  0.0 111.8 jit_solution(10146788711843972857)
XLA Ops:
  0.6 0.0 copy-start.1
  0.6 0.7 copy-done.1
  1.3 0.0 copy-start
  1.3 0.9 copy-done
  2.3 108.1 %shard_map.41 = (bf16[4,2,128,128]{3,2,1,0:T(8,128)(2,1)S(1)}, bf16[4,2,128,128]{3,2,1,0:T(8,128)(2,1)S(1)}) custom-call(bf16[1024,128]{1,0:T(8,128)(2,1)S(1)} %bitcast.2, s32[2,4]{1,0:T(2,128)S(1)} %bitcast.3), custom_call_target="tpu_custom_call" | custom-call | tf_op jit(solution)/shard_map/pallas_call | solution.py:329
  110.4 0.7 copy.6
  111.1 0.7 copy.7
Async XLA Ops:
  0.6 0.7 copy-start.1
  1.3 0.9 copy-start

commit v3 on v2

--- a/solution.py
+++ b/solution.py
@@ -11,7 +11,7 @@
 LINES = 16
 BLOCKS = 8
 BS = 128
-GROUP = 4
+GROUP = 7
 HEAD = 16
 ROWS = BLOCKS * BS
 MESH = pl.DeviceIdType.MESH
@@ -26,13 +26,13 @@
 
 UP = [(1, q, d) for d in (1, 2, 3) for q in (0, 1, 2, 3)] + [(1, q, 4) for q in (0, 1)]
 DOWN = [(-1, q, d) for d in (1, 2, 3) for q in (2, 3, 0, 1)] + [(-1, q, 4) for q in (2, 3)]
-CROSS = [("c", 1, 0)] + [("c", s, d) for d in (1, 2, 3, 4) for s in (1, -1)]
+CROSS = [("c", 1, 0)] + [("c", s, d) for d in (1, 2, 3, 4, 5) for s in (1, -1)]
 COL_ID = {key: n for n, key in enumerate(UP + DOWN + CROSS)}
 
 
 def kernel(
     tiles, pattern, sign_out, square_out,
-    left, right, mid, loc, acc, pv, table, used,
+    left, right, mid, loc, acc, codes, pv, table, used,
     tsem, psem, rsend, rrecv, csend, crecv,
 ):
     row, col = lax.axis_index("row"), lax.axis_index("col")
@@ -79,9 +79,10 @@
     def col_copy(it, key, sending):
         sign, d = key[-3] if key[0] != "c" else key[1], key[-1]
         if key[0] == "c":
-            ref_col = col_at(-sign * d, sending)
+            ref_col = col_at(-sign * min(d, 4), sending)
             target = col_at(0, False)
-            lo, hi = (0, 4) if d < 4 else ((0, 2) if sign == 1 else (2, 4))
+            lo = d - 4 if sign == 1 else d - 2
+            lo, hi = (0, 4) if d < 4 else (lo, lo + 1)
         else:
             ref_col = col_at(-sign * (d - 1 if sending else d))
             target = col_at(sign)
@@ -106,8 +107,8 @@
                 sign, q, d = key
                 if (sign, q, d + 1) in COL_ID:
                     col_copy(it, (sign, q, d + 1), True).start()
-                if n % 4 == 3 or n == 13:
-                    col_copy(it, ("c", sign, d), True).start()
+                if n % 4 == 3 or n >= 12:
+                    col_copy(it, ("c", sign, d + (n == 13)), True).start()
 
     def cross_wait(it, *ds):
         for key in CROSS:
@@ -166,16 +167,17 @@
 
     def decode(tile):
         at = lax.broadcasted_iota(jnp.int32, (HEAD, BS), 0)
-        entry = tile.astype(jnp.float32).astype(jnp.int32) + 1
-        code = jnp.where(at < BLOCKS, entry << (3 * jnp.minimum(at, BLOCKS - 1)), 0)
-        return jnp.sum(code, axis=0, keepdims=True)
-
-    def make_table():
-        for r in range(LINES):
-            pv[0, r : r + 1] = decode(right[0, r, 0:HEAD])
-            pv[1, r : r + 1] = decode(left[0, r, 0:HEAD])
-        theirs, mine = pv[0], pv[1]
-        own = jnp.broadcast_to(decode(left[0, col, 0:HEAD]), (LINES, BS))
+        weight = jnp.where(at < BLOCKS, 1 << (3 * jnp.minimum(at, BLOCKS - 1)), 0).astype(jnp.float32)
+        return jnp.sum(tile.astype(jnp.float32) * weight, axis=0, keepdims=True)
+
+    def make_table(rows, cols):
+        for r in rows:
+            codes[0, pl.ds(r, 1)] = decode(right[0, r, 0:HEAD])
+        for c in cols:
+            codes[1, pl.ds(c, 1)] = decode(left[0, c, 0:HEAD])
+        ones = sum(1 << (3 * n) for n in range(BLOCKS))
+        theirs, mine = codes[0].astype(jnp.int32) + ones, codes[1].astype(jnp.int32) + ones
+        own = jnp.broadcast_to(decode(left[0, col, 0:HEAD]), (LINES, BS)).astype(jnp.int32) + ones
         lane = lax.broadcasted_iota(jnp.int32, (LINES, BS), 1) & 15
         i, s, t = lane >> 2, (lane >> 1) & 1, lane & 1
         k = ((mine >> (6 * i + 3 * s)) & 7) - 1
@@ -183,13 +185,30 @@
         pair = theirs >> (6 * at_k)
         j = (own >> (6 * i + 3 * t)) & 7
         found = jnp.where((pair & 7) == j, 2 * at_k, jnp.where(((pair >> 3) & 7) == j, 2 * at_k + 1, BLOCKS))
-        pv[2] = jnp.where((k >= 0) & (j > 0), found, BLOCKS)
-        pv[3] = j
-        copies = [pltpu.make_async_copy(pv.at[2 + n], (table, used)[n], psem.at[n]) for n in (0, 1)]
+        pv[0] = jnp.where((k >= 0) & (j > 0), found, BLOCKS)
+        pv[1] = j
+        copies = [pltpu.make_async_copy(pv.at[n], (table, used)[n], psem.at[n]) for n in (0, 1)]
         for copy in copies:
             copy.start()
         for copy in copies:
             copy.wait()
+
+    def order_pieces():
+        ranks = []
+        for r in range(LINES):
+            dx, dy, dz = apart(r // SIDE, x, SIDE), apart(r % SIDE, y, SIDE), apart(r // 2, z, RING)
+            mine = core == r % 2
+            soon = (dx + dy <= 2) & ((dz <= 2) | (mine & (dz <= 3)))
+            later = (dx + dy <= 3) & ((dz <= 2) | mine)
+            ranks.append((soon.astype(jnp.int32), later.astype(jnp.int32)))
+        first, second, third = jnp.int32(0), sum(soon for soon, _ in ranks), jnp.int32(LINES - 1)
+        order = [jnp.int32(0)] * 4
+        for r, (soon, later) in enumerate(ranks):
+            at = jnp.where(soon == 1, first, jnp.where(later == 1, second, third))
+            first, second, third = first + soon, second + later - soon, third - (1 - later)
+            for n in range(LINES):
+                order[n // 4] = order[n // 4] + jnp.where(at == n, r * 16 ** (n % 4), 0)
+        return [lax.rem(lax.div(order[n // 4], 16 ** (n % 4)), 16) for n in range(LINES)]
 
     barrier = pltpu.get_barrier_semaphore()
     for peer in (
@@ -210,28 +229,8 @@
     for n in range(BLOCKS):
         entry = jnp.broadcast_to(pattern[n % 2 : n % 2 + 1, n // 2 : n // 2 + 1], (HEAD, BS)).astype(jnp.float32)
         head = jnp.where(n_row == n, entry, head)
-    for it in range(ITERS):
-        right[it, row, 0:HEAD] = head.astype(jnp.bfloat16)
-        left[it, col, 0:HEAD] = head.astype(jnp.bfloat16)
-    for k in range(GROUP):
-        loc[k, BLOCKS] = jnp.zeros((BS, BS), jnp.bfloat16)
-
-    early, order = jnp.int32(0), [jnp.int32(0)] * (LINES // GROUP)
-    for r in range(LINES):
-        dx, dy, dz = apart(r // SIDE, x, SIDE), apart(r % SIDE, y, SIDE), apart(r // 2, z, RING)
-        soon = jnp.where((dx + dy <= 2) & (dz <= 3), 1, 0)
-        at = jnp.where(soon == 1, early, LINES - 1 - r + early)
-        early = early + soon
-        for k in range(LINES // GROUP):
-            for j in range(GROUP):
-                order[k] = order[k] + jnp.where(at == k * GROUP + j, r * 16**j, 0)
-
-    def group(k):
-        word = order[0]
-        for n in range(1, LINES // GROUP):
-            word = jnp.where(k == n, order[n], word)
-        return [lax.rem(lax.div(word, 16**j), 16) for j in range(GROUP)]
-
+    right[0, row, 0:HEAD] = head.astype(jnp.bfloat16)
+    left[0, col, 0:HEAD] = head.astype(jnp.bfloat16)
     for copy in fetch:
         copy.wait()
     pl.semaphore_wait(barrier, 7)
@@ -243,43 +242,63 @@
         row_start(g)
         col_start(it)
         acc[...] = jnp.zeros_like(acc)
+        order = order_pieces()
+
+        @pl.when(it == 0)
+        def _():
+            codes[...] = jnp.zeros_like(codes)
+            for k in range(GROUP):
+                loc[k, BLOCKS] = jnp.zeros((BS, BS), jnp.bfloat16)
+            right[1, row, 0:HEAD] = right[0, row, 0:HEAD]
+            left[1, col, 0:HEAD] = left[0, col, 0:HEAD]
+
         col_event(it, 0, 1)
         row_e1(g)
         col_event(it, 2, 3)
         row_e3(g)
         col_event(it, 4, 5, 6)
+        row_fan(g, 0)
         row_fan(g, -1)
         col_event(it, 7, 8)
         row_fan(g, 1)
         col_event(it, 9, 10, 11)
-        row_fan(g, 0)
         row_fan(g, 2)
-        col_event(it, 12, 13)
         row_last(g, 0)
-        cross_wait(it, 0, 1, 2, 3)
-
-        @pl.when(it > 0)
-        def _():
-            @pl.loop(0, 2)
-            def _(k):
-                pieces(it, 0, group(k))
-
-        row_last(g, -1, 1, 2)
-        cross_wait(it, 4)
+        cross_wait(it, 0, 1, 2)
 
         @pl.when(it == 0)
         def _():
-            make_table()
-
-        @pl.loop(jnp.where(it == 0, 0, 2), 4)
-        def _(k):
-            pieces(it, 0, group(k))
+            make_table(
+                [row_at(dx, dy) for dx in (-1, 0, 1, 2) for dy in (-1, 0, 1, 2) if abs(dx) + abs(dy) <= 2],
+                [col_at(dz) for dz in range(-3, 4)] + [col_at(dz, False) for dz in range(-2, 3)],
+            )
+
+        pieces(it, 0, order[:7])
+        col_event(it, 12)
+        row_last(g, -1)
+        col_event(it, 13)
+        row_last(g, 1)
+
+        @pl.when(it == 0)
+        def _():
+            make_table([row_at(2, -1), row_at(2, 1), row_at(-1, 2), row_at(1, 2)], [col_at(4)])
+
+        pieces(it, 0, order[7:12])
+        row_last(g, 2)
+        cross_wait(it, 3, 4, 5)
+
+        @pl.when(it == 0)
+        def _():
+            make_table([row_at(2, 2)], [col_at(dz, False) for dz in (-3, 3, 4)])
+
+        pieces(it, 0, order[12:])
 
         scale = 1.0 / (2.0 * 2 * LINES * BS)
         for i in range(4):
             for t in range(2):
-                new = acc[i, :, t * BS : (t + 1) * BS] * scale
-                mid[it, row, pl.ds((2 * i + t) * BS, BS)] = new.astype(jnp.bfloat16)
+                new = (acc[i, :, t * BS : (t + 1) * BS] * scale).astype(jnp.bfloat16)
+                mid[it, row, pl.ds((2 * i + t) * BS, BS)] = new
+                square_out[i, t] = new
 
         row_start(m)
         acc[...] = jnp.zeros_like(acc)
@@ -300,22 +319,23 @@
         row_last(m, 2)
         pieces(it, 1, [row_at(2, 2)])
 
-        for i in range(4):
-            for t in range(2):
-                s = left[it, col, block(2 * i + t)].astype(jnp.float32)
-                new = 1.5 * s - 0.5 * acc[i, :, t * BS : (t + 1) * BS]
-                keep = used[0, 4 * i + t] > 0
-                sign_out[i, t] = jnp.where(keep, new, 0.0).astype(jnp.bfloat16)
+        def new_sign(i, t):
+            s = left[it, col, block(2 * i + t)].astype(jnp.float32)
+            new = 1.5 * s - 0.5 * acc[i, :, t * BS : (t + 1) * BS]
+            return jnp.where(used[0, 4 * i + t] > 0, new, 0.0).astype(jnp.bfloat16)
 
         @pl.when(it < ITERS - 1)
         def _():
             for n in range(BLOCKS):
-                now = sign_out[n // 2, n % 2]
+                now = new_sign(n // 2, n % 2)
+                right[it + 1, row, block(n)] = now
                 left[it + 1, col, block(n)] = now
-                right[it + 1, row, block(n)] = now
-
-    for n in range(BLOCKS):
-        square_out[n // 2, n % 2] = mid[ITERS - 1, row, pl.ds(n * BS, BS)]
+
+        @pl.when(it == ITERS - 1)
+        def _():
+            for n in range(BLOCKS):
+                sign_out[n // 2, n % 2] = new_sign(n // 2, n % 2)
+
     for it in range(ITERS):
         sent(right, rsend.at[it, 0])
         sent(mid, rsend.at[it, 1])
@@ -337,7 +357,8 @@
             pltpu.VMEM((ITERS, LINES, ROWS, BS), jnp.bfloat16),
             pltpu.VMEM((GROUP, BLOCKS + 1, BS, BS), jnp.bfloat16),
             pltpu.VMEM((4, BS, 2 * BS), jnp.float32),
-            pltpu.VMEM((4, LINES, BS), jnp.int32),
+            pltpu.VMEM((2, LINES, BS), jnp.float32),
+            pltpu.VMEM((2, LINES, BS), jnp.int32),
             pltpu.SMEM((LINES, BS), jnp.int32),
             pltpu.SMEM((LINES, BS), jnp.int32),
             dma((2,)),

time: 112 us -> 111 us (level)
  Pallas kernels: 108 us -> 106 us
    pallas_call x1, Pallas kernels: 108 us -> 106 us  [shards(): pl.pallas_call(kernel, out_shape=(shape, shape), in_specs=[pl.BlockSpec(m...]
where the time goes in v3:
time: 111 us; the launch traced here: 110 us
  Pallas kernels  106 us (95%)
  local copies, waits for them, and re-layouts  3.03 us (3%)
    pallas_call x1, Pallas kernels, shards(): pl.pallas_call(kernel, out_shape=(shape, shape), in_specs=[pl.BlockSpec(m...  106 us
    unnamed x6, local copies, waits for them, and re-layouts  3.03 us

profile of v3, /device:TPU:2, one launch (start us, length us, event | category | flops | bytes accessed | tf_op | source)
XLA Modules:
  0.0 109.7 jit_solution(2454741517346462474)
XLA Ops:
  0.6 0.0 copy-start.1
  0.6 0.7 copy-done.1
  1.3 0.0 copy-start
  1.3 0.9 copy-done
  2.3 106.1 %shard_map.41 = (bf16[4,2,128,128]{3,2,1,0:T(8,128)(2,1)S(1)}, bf16[4,2,128,128]{3,2,1,0:T(8,128)(2,1)S(1)}) custom-call(bf16[1024,128]{1,0:T(8,128)(2,1)S(1)} %bitcast.2, s32[2,4]{1,0:T(2,128)S(1)} %bitcast.3), custom_call_target="tpu_custom_call" | custom-call | tf_op jit(solution)/shard_map/pallas_call | solution.py:349
  108.3 0.7 copy.6
  109.0 0.7 copy.7
Async XLA Ops:
  0.6 0.7 copy-start.1
  1.3 0.9 copy-start

commit v4 on v3

--- a/solution.py
+++ b/solution.py
@@ -31,10 +31,11 @@
 
 
 def kernel(
-    tiles, pattern, sign_out, square_out,
+    tiles, pattern, out,
     left, right, mid, loc, acc, codes, pv, table, used,
     tsem, psem, rsend, rrecv, csend, crecv,
 ):
+    sign_out, square_out = out.at[0], out.at[1]
     row, col = lax.axis_index("row"), lax.axis_index("col")
     x, y = lax.div(row, SIDE), lax.rem(row, SIDE)
     z, core = lax.div(col, 2), lax.rem(col, 2)
@@ -252,19 +253,19 @@
             right[1, row, 0:HEAD] = right[0, row, 0:HEAD]
             left[1, col, 0:HEAD] = left[0, col, 0:HEAD]
 
-        col_event(it, 0, 1)
+        col_event(it, 0,1)
         row_e1(g)
-        col_event(it, 2, 3)
+        col_event(it, 2,3)
+        row_fan(g, 0)
         row_e3(g)
-        col_event(it, 4, 5, 6)
-        row_fan(g, 0)
+        col_event(it, 4,5,6)
         row_fan(g, -1)
-        col_event(it, 7, 8)
+        col_event(it, 7,8)
         row_fan(g, 1)
-        col_event(it, 9, 10, 11)
+        col_event(it, 9,10,11)
         row_fan(g, 2)
         row_last(g, 0)
-        cross_wait(it, 0, 1, 2)
+        cross_wait(it, 0,1,2)
 
         @pl.when(it == 0)
         def _():
@@ -273,8 +274,8 @@
                 [col_at(dz) for dz in range(-3, 4)] + [col_at(dz, False) for dz in range(-2, 3)],
             )
 
+        col_event(it, 12)
         pieces(it, 0, order[:7])
-        col_event(it, 12)
         row_last(g, -1)
         col_event(it, 13)
         row_last(g, 1)
@@ -346,11 +347,11 @@
     shape = jax.ShapeDtypeStruct(tiles.shape, tiles.dtype)
     vmem = pl.BlockSpec(memory_space=pltpu.VMEM)
     dma = pltpu.SemaphoreType.DMA
-    return pl.pallas_call(
+    both = pl.pallas_call(
         kernel,
-        out_shape=(shape, shape),
+        out_shape=jax.ShapeDtypeStruct((2,) + tiles.shape, tiles.dtype),
         in_specs=[pl.BlockSpec(memory_space=pltpu.HBM), vmem],
-        out_specs=(vmem, vmem),
+        out_specs=vmem,
         scratch_shapes=[
             pltpu.VMEM((ITERS, LINES, HEAD + ROWS, BS), jnp.bfloat16),
             pltpu.VMEM((ITERS, LINES, HEAD + ROWS, BS), jnp.bfloat16),
@@ -372,6 +373,7 @@
             collective_id=0, has_side_effects=True, vmem_limit_bytes=48 * 1024 * 1024
         ),
     )(tiles.reshape(ROWS, BS), pattern.T)
+    return both[0], both[1]
 
 
 def solution(mesh):

time: 111 us -> 110 us (level)
    unnamed x6 -> x4, local copies, waits for them, and re-layouts: 3.03 us -> 1.62 us
where the time goes in v4:
time: 110 us; the launch traced here: 109 us
  Pallas kernels  106 us (96%)
  local copies, waits for them, and re-layouts  2.46 us (2%)
    pallas_call x1, Pallas kernels, shards(): pl.pallas_call(kernel, out_shape=jax.ShapeDtypeStruct((2,) + tiles.shape,...  106 us

profile of v4, /device:TPU:2, one launch (start us, length us, event | category | flops | bytes accessed | tf_op | source)
XLA Modules:
  0.0 109.4 jit_solution(8421912224146899787)
XLA Ops:
  0.6 0.0 copy-start.1
  0.6 0.7 copy-done.1
  1.3 0.0 copy-start
  1.3 0.9 copy-done
  2.3 106.3 %shard_map.41 = bf16[2,4,2,128,128]{4,3,2,1,0:T(8,128)(2,1)S(1)} custom-call(bf16[1024,128]{1,0:T(8,128)(2,1)S(1)} %bitcast.6, s32[2,4]{1,0:T(2,128)S(1)} %bitcast.7), custom_call_target="tpu_custom_call" | custom-call | tf_op jit(solution)/shard_map/pallas_call | solution.py:350
  108.6 0.8 slice_bitcast_fusion
Async XLA Ops:
  0.6 0.7 copy-start.1
  1.3 0.9 copy-start

commit v5 on v4

--- a/solution.py
+++ b/solution.py
@@ -116,8 +116,9 @@
             if key[2] in ds:
                 col_copy(it, key, False).wait_recv()
 
-    def row_start(g):
+    def row_start(g, ready=lambda h: None):
         for h in (0, 1):
+            ready(h)
             row_send(g, (h, -1, 0, "w"), (h, 1, 0, "w"))
         for h in (1, 0):
             row_send(g, (h, 0, -1, "w"), (h, 0, 1, "w"))
@@ -295,13 +296,14 @@
         pieces(it, 0, order[12:])
 
         scale = 1.0 / (2.0 * 2 * LINES * BS)
-        for i in range(4):
-            for t in range(2):
-                new = (acc[i, :, t * BS : (t + 1) * BS] * scale).astype(jnp.bfloat16)
-                mid[it, row, pl.ds((2 * i + t) * BS, BS)] = new
-                square_out[i, t] = new
-
-        row_start(m)
+        def square_half(h):
+            for i in (2 * h, 2 * h + 1):
+                for t in range(2):
+                    new = (acc[i, :, t * BS : (t + 1) * BS] * scale).astype(jnp.bfloat16)
+                    mid[it, row, pl.ds((2 * i + t) * BS, BS)] = new
+                    square_out[i, t] = new
+
+        row_start(m, square_half)
         acc[...] = jnp.zeros_like(acc)
         row_e1(m)
         row_e3(m)

time: 110 us -> 110 us (level)
  no operation moved by 1% of the time
where the time goes in v5:
time: 110 us; the launch traced here: 109 us
  Pallas kernels  106 us (96%)
  local copies, waits for them, and re-layouts  2.46 us (2%)
    pallas_call x1, Pallas kernels, shards(): pl.pallas_call(kernel, out_shape=jax.ShapeDtypeStruct((2,) + tiles.shape,...  106 us

profile of v5, /device:TPU:2, one launch (start us, length us, event | category | flops | bytes accessed | tf_op | source)
XLA Modules:
  0.0 109.4 jit_solution(18028238445732409199)
XLA Ops:
  0.6 0.0 copy-start.1
  0.6 0.7 copy-done.1
  1.3 0.0 copy-start
  1.3 0.9 copy-done
  2.3 106.3 %shard_map.41 = bf16[2,4,2,128,128]{4,3,2,1,0:T(8,128)(2,1)S(1)} custom-call(bf16[1024,128]{1,0:T(8,128)(2,1)S(1)} %bitcast.6, s32[2,4]{1,0:T(2,128)S(1)} %bitcast.7), custom_call_target="tpu_custom_call" | custom-call | tf_op jit(solution)/shard_map/pallas_call | solution.py:352
  108.6 0.8 slice_bitcast_fusion
Async XLA Ops:
  0.6 0.7 copy-start.1
  1.3 0.9 copy-start

commit v6 on v5

--- a/solution.py
+++ b/solution.py
@@ -241,7 +241,10 @@
     def _(it):
         g, m = (it, 0), (it, 1)
 
-        row_start(g)
+        @pl.when(it == 0)
+        def _():
+            row_start(g)
+
         col_start(it)
         acc[...] = jnp.zeros_like(acc)
         order = order_pieces()
@@ -329,10 +332,13 @@
 
         @pl.when(it < ITERS - 1)
         def _():
-            for n in range(BLOCKS):
-                now = new_sign(n // 2, n % 2)
-                right[it + 1, row, block(n)] = now
-                left[it + 1, col, block(n)] = now
+            def sign_half(h):
+                for n in range(4 * h, 4 * h + 4):
+                    now = new_sign(n // 2, n % 2)
+                    right[it + 1, row, block(n)] = now
+                    left[it + 1, col, block(n)] = now
+
+            row_start((it + 1, 0), sign_half)
 
         @pl.when(it == ITERS - 1)
         def _():

time: 110 us -> 110 us (level)
  no operation moved by 1% of the time
where the time goes in v6:
time: 110 us; the launch traced here: 109 us
  Pallas kernels  106 us (96%)
  local copies, waits for them, and re-layouts  2.46 us (2%)
    pallas_call x1, Pallas kernels, shards(): pl.pallas_call(kernel, out_shape=jax.ShapeDtypeStruct((2,) + tiles.shape,...  106 us

profile of v6, /device:TPU:2, one launch (start us, length us, event | category | flops | bytes accessed | tf_op | source)
XLA Modules:
  0.0 109.4 jit_solution(9671802476827569868)
XLA Ops:
  0.6 0.0 copy-start.1
  0.6 0.7 copy-done.1
  1.3 0.0 copy-start
  1.3 0.9 copy-done
  2.3 106.3 %shard_map.41 = bf16[2,4,2,128,128]{4,3,2,1,0:T(8,128)(2,1)S(1)} custom-call(bf16[1024,128]{1,0:T(8,128)(2,1)S(1)} %bitcast.6, s32[2,4]{1,0:T(2,128)S(1)} %bitcast.7), custom_call_target="tpu_custom_call" | custom-call | tf_op jit(solution)/shard_map/pallas_call | solution.py:358
  108.6 0.8 slice_bitcast_fusion
Async XLA Ops:
  0.6 0.7 copy-start.1
  1.3 0.9 copy-start
